TPU v7x, 512 devices: a whole 4x8x8 slice. The times are simulated.
512 devices in a mesh: seq: 16 (over x_hi, y), group: 32 (over z, x_lo, core).
Axes of the slice: x: 4 (x_hi: 2, x_lo: 2; x = x_hi * 2 + x_lo), y: 8, z: 8, core: 2. Of those that a mesh axis runs over, the one named last changes fastest.
Arguments:
- query_proj: bfloat16 [32, 1024, 8192], P('group', 'seq'), may hold values from -6 to 6
- key_proj: bfloat16 [32, 1024, 1024], P('group', 'seq'), may hold values from -6 to 6
- value_proj: bfloat16 [32, 1024, 1024], P('group', 'seq'), may hold values from -6 to 6
- query_gain: float32 [128], replicated, may hold values from 1 to 5.5, as said below
- key_gain: float32 [128], replicated, may hold values from 1 to 5.5, as said below
- doc_lengths: int32 [32, 4], P('group'), may hold values from 1 to 512, 1024 in all within a row
Outputs:
- attended: bfloat16 [32, 1024, 8192], P('group', 'seq')
- cache: bfloat16 [16, 32, 32, 1, 16, 256], P('seq', 'group')
Inputs may be any that keep to these rules, and one draw needn't show every extreme that they name: `query_gain`: a gain for each of the 128 features. `key_gain`: a gain for each of the 128 features.
All inputs are finite; a program needn't handle non-finite values.
Results may differ from a plain program's by a relative error of at most 0.0045.
The roundings to bfloat16 on the way count: a program that leaves them out, or rounds other values in their place, can miss the bound.
Values may be sent and summed in bfloat16 or wider, within the bound.
No kernel may reach another device: no remote copies, remote signals or barrier semaphores. Data moves between devices by JAX's collectives and lax.ppermute only.
A program may use at most 64 MiB of HBM per device.

v0:
```python
import math
import jax
import jax.numpy as jnp
from jax import lax
from jax.sharding import PartitionSpec as P

PAGE = 16
NORM_EPS = 1e-06
ROPE_BASE = 1000000.0
MASKED = -1e30


def token_starts(lengths, count):
    doc_ends = jnp.cumsum(lengths)
    token_index = jnp.arange(count, dtype=jnp.int32)
    passed = (doc_ends[None, :] <= token_index[:, None]).astype(jnp.int32)
    return jnp.sum(passed * lengths[None, :], axis=1)


def rope_tables(positions, head_width):
    half_width = head_width // 2
    exponent = jnp.arange(half_width, dtype=jnp.float32) * (-2.0 / head_width)
    inverse = jnp.power(jnp.float32(ROPE_BASE), exponent)
    angles = positions.astype(jnp.float32)[:, None] * inverse[None, :]
    return (jnp.cos(angles), jnp.sin(angles))


def norm_rope(heads_in, gain, cosine, sine):
    values_f = heads_in.astype(jnp.float32)
    inv_rms = lax.rsqrt(jnp.mean(values_f * values_f, axis=-1, keepdims=True) + NORM_EPS)
    normed = values_f * inv_rms * gain
    half_width = heads_in.shape[-1] // 2
    front = normed[..., :half_width]
    back_half = normed[..., half_width:]
    cos_b = cosine[:, None, :]
    sin_b = sine[:, None, :]
    rotated = jnp.concatenate(
        [front * cos_b - back_half * sin_b, back_half * cos_b + front * sin_b], axis=-1
    )
    return rotated.astype(jnp.bfloat16)


def attend(q_all, kv_all, starts, head_width):
    token_count = q_all.shape[0]
    entry_count = q_all.shape[1]
    head_count = q_all.shape[2]
    block_size = math.gcd(token_count, 512)
    block_count = token_count // block_size
    score_scale = 1.0 / math.sqrt(head_width)
    block_range = jnp.arange(block_size, dtype=jnp.int32)

    def one_block(block_id):
        q_first = block_id * block_size
        q_block = lax.dynamic_slice_in_dim(q_all, q_first, block_size, 0)
        q_index = q_first + block_range
        q_start = lax.dynamic_slice_in_dim(starts, q_first, block_size, 0)

        def key_step(key_block, carry):
            run_top, denom, accum = carry
            kv_block = lax.dynamic_slice_in_dim(kv_all, key_block * block_size, block_size, 0)
            k_index = key_block * block_size + block_range
            scores = (
                jnp.einsum(
                    "qend,ked->enqk",
                    q_block,
                    kv_block[..., :head_width],
                    preferred_element_type=jnp.float32,
                )
                * score_scale
            )
            visible = (k_index[None, :] <= q_index[:, None]) & (
                k_index[None, :] >= q_start[:, None]
            )
            scores = jnp.where(visible, scores, MASKED)
            new_top = jnp.maximum(run_top, jnp.max(scores, axis=-1))
            factor = jnp.exp(run_top - new_top)
            weights = jnp.where(visible, jnp.exp(scores - new_top[..., None]), 0.0)
            denom = denom * factor + jnp.sum(weights, axis=-1)
            update = jnp.einsum(
                "enqk,ked->enqd",
                weights.astype(jnp.bfloat16),
                kv_block[..., head_width:],
                preferred_element_type=jnp.float32,
            )
            accum = accum * factor[..., None] + update
            return (new_top, denom, accum)

        start_top = jnp.full((entry_count, head_count, block_size), MASKED, jnp.float32)
        start_sum = jnp.zeros((entry_count, head_count, block_size), jnp.float32)
        start_acc = jnp.zeros((entry_count, head_count, block_size, head_width), jnp.float32)
        run_top, denom, accum = lax.fori_loop(
            0, block_id + 1, key_step, (start_top, start_sum, start_acc)
        )
        return (accum / denom[..., None]).astype(jnp.bfloat16).transpose(2, 0, 1, 3)

    blocks = lax.map(one_block, jnp.arange(block_count, dtype=jnp.int32))
    return blocks.reshape(token_count, entry_count, head_count, head_width)


def page_cache(kv_all, entry_first, repeat):
    token_count, entry_count, pair_width = kv_all.shape
    slots = lax.axis_size("group")
    pages = token_count // (PAGE * repeat * slots)
    paged = kv_all.reshape(pages, repeat, slots, PAGE, entry_count, pair_width)
    copy_class = (entry_first + 0) % repeat
    chosen = lax.dynamic_index_in_dim(paged, copy_class, 1, False)
    picked = [chosen[:, :, :, 0, :]]
    outgoing = jnp.stack(picked)[:, None]
    moved = lax.all_to_all(outgoing, "group", split_axis=3, concat_axis=1, tiled=True)
    return moved.reshape(entry_count, 1, slots, pages, PAGE, pair_width)


def body(query_proj, key_proj, value_proj, query_gain, key_gain, doc_lengths):
    seq_count = lax.axis_size("seq")
    head_width = query_gain.shape[0]
    row_count = query_proj.shape[1]
    q_heads = query_proj.shape[2] // head_width
    kv_heads = key_proj.shape[2] // head_width
    token_count = row_count * seq_count
    entries = max(kv_heads, seq_count)
    repeat = entries // kv_heads
    local_entries = entries // seq_count
    sharing = q_heads // entries
    starts = token_starts(doc_lengths[0], token_count)
    first_row = lax.axis_index("seq") * row_count
    own_index = first_row + jnp.arange(row_count, dtype=jnp.int32)
    own_starts = lax.dynamic_slice_in_dim(starts, first_row, row_count, 0)
    cosine, sine = rope_tables(own_index - own_starts, head_width)
    q_rot = norm_rope(
        query_proj[0].reshape(row_count, q_heads, head_width), query_gain, cosine, sine
    )
    k_rot = norm_rope(key_proj[0].reshape(row_count, kv_heads, head_width), key_gain, cosine, sine)
    pairs = jnp.concatenate(
        [k_rot, value_proj[0].reshape(row_count, kv_heads, head_width)], axis=-1
    )
    spread = jnp.repeat(pairs, repeat, axis=1).reshape(
        row_count, seq_count, local_entries, 2 * head_width
    )
    q_split = q_rot.reshape(row_count, seq_count, local_entries, sharing, head_width)
    entry_first = lax.axis_index("seq") * local_entries
    q_got, kv_got = (
        lax.all_to_all(q_split, "seq", split_axis=1, concat_axis=0, tiled=True),
        lax.all_to_all(spread, "seq", split_axis=1, concat_axis=0, tiled=True),
    )
    q_all = q_got.reshape(token_count, local_entries, sharing, head_width)
    kv_all = kv_got.reshape(token_count, local_entries, 2 * head_width)
    mixed = attend(q_all, kv_all, starts, head_width)
    back = lax.all_to_all(
        mixed.reshape(token_count, 1, local_entries, sharing, head_width),
        "seq",
        split_axis=0,
        concat_axis=1,
        tiled=True,
    )
    cache = page_cache(kv_all, entry_first, repeat)
    attended = back.reshape(1, row_count, q_heads * head_width)
    return (attended, cache)


def solution(mesh):
    in_specs = (
        P("group", "seq", None),
        P("group", "seq", None),
        P("group", "seq", None),
        P(),
        P(),
        P("group", None),
    )
    out_specs = (P("group", "seq", None), P("seq", "group", None, None, None, None))
    return jax.shard_map(body, mesh=mesh, in_specs=in_specs, out_specs=out_specs, check_vma=False)
```

profile of v0, /device:TPU:2, one launch (start us, length us, event | category | flops | bytes accessed | tf_op | source)
XLA Modules:
  0.0 150.2 jit_solution(15361947048695826945)
XLA Ops:
  0.7 0.9 reduce-window.8
  1.6 0.9 convert_bitcast_fusion.1
  2.9 0.9 copy.72
  3.8 0.7 select_reduce_fusion
  4.6 0.2 multiply_cosine_fusion
  4.8 0.8 multiply_multiply_fusion.1
  5.6 0.2 subtract_convert_fusion.1
  5.8 0.1 pad_maximum_fusion
  6.0 0.9 broadcast_in_dim.18
  6.8 8.8 %all-to-all-start.1 = ((bf16[64,16,1,256]{3,0,2,1:T(8,128)(2,1)}), bf16[64,16,1,256]{3,0,2,1:T(8,128)(2,1)S(1)}, u32[]{:S(2)}, u32[]{:S(2)}) async-start(bf16[64,16,1,256]{3,0,2,1:T(8,128)(2,1)} %bitcast.22), calls=%async_computation.1 | async-start | bytes 1048576 | tf_op jit(solution)/shard_map/all_to_all | solution.py:143
  15.6 0.1 convert_bitcast_fusion
  15.8 0.4 copy.70
  16.2 0.6 multiply_reduce_fusion
  16.8 0.9 multiply_multiply_fusion
  17.7 0.9 subtract_convert_fusion
  18.6 0.7 copy.55
  19.3 0.7 copy.56
  20.0 1.6 %maximum_bitcast_fusion = bf16[64,16,1,4,128]{4,0,3,2,1:T(8,128)(2,1)} fusion(bf16[64,16,1,4,64]{4,0,3,1,2:T(8,128)(2,1)S(1)} %bitcast.144, bf16[64,16,1,4,64]{4,0,3,1,2:T(8,128)(2,1)S(1)} %bitcast.143), kind=kLoop, calls=%fused_computation.35 | loop fusion | flops 2097152 | bytes 2097152 | tf_op jit(solution)/shard_map/concatenate | solution.py:37
  21.6 11.3 %all-to-all-done.1 = bf16[64,16,1,256]{3,0,2,1:T(8,128)(2,1)S(1)} async-done(((bf16[64,16,1,256]{3,0,2,1:T(8,128)(2,1)}), bf16[64,16,1,256]{3,0,2,1:T(8,128)(2,1)S(1)}, u32[]{:S(2)}, u32[]{:S(2)}) %all-to-all-start.1) | async-done | bytes 524320 | tf_op jit(solution)/shard_map/all_to_all | solution.py:143
  32.8 4.5 %all-to-all-start = ((bf16[64,16,1,4,128]{4,0,3,2,1:T(8,128)(2,1)}), bf16[64,16,1,4,128]{4,0,3,2,1:T(8,128)(2,1)S(1)}, u32[]{:S(2)}, u32[]{:S(2)}) async-start(bf16[64,16,1,4,128]{4,0,3,2,1:T(8,128)(2,1)} %maximum_bitcast_fusion), calls=%async_computation | async-start | bytes 2097152 | tf_op jit(solution)/shard_map/all_to_all | solution.py:142
  37.4 0.7 dynamic-slice_bitcast_fusion.4
  38.1 26.5 %all-to-all-done = bf16[64,16,1,4,128]{4,0,3,2,1:T(8,128)(2,1)S(1)} async-done(((bf16[64,16,1,4,128]{4,0,3,2,1:T(8,128)(2,1)}), bf16[64,16,1,4,128]{4,0,3,2,1:T(8,128)(2,1)S(1)}, u32[]{:S(2)}, u32[]{:S(2)}) %all-to-all-start) | async-done | bytes 1048608 | tf_op jit(solution)/shard_map/all_to_all | solution.py:142
  64.6 12.0 %all-to-all-start.3 = ((bf16[1,1,1,32,16,256]{5,4,2,1,0,3:T(8,128)(2,1)}), bf16[1,1,1,32,16,256]{5,4,2,1,0,3:T(8,128)(2,1)}, u32[]{:S(2)}, u32[]{:S(2)}) async-start(bf16[1,1,1,32,16,256]{5,4,2,1,0,3:T(8,128)(2,1)} %dynamic-slice_bitcast_fusion.4), calls=%async_computation.3 | async-start | bytes 524288 | tf_op jit(solution)/shard_map/all_to_all | solution.py:109
  76.7 32.0 %while.29 = (s32[]{:T(128)}, bf16[2,512,1,4,128]{4,1,0,3,2:T(8,128)(2,1)}, s32[2]{0:T(128)S(1)}, bf16[1024,1,4,128]{3,0,2,1:T(8,128)(2,1)S(1)}, s32[1024]{0:T(10...) while((s32[]{:T(128)}, ...), condition=%wide.region_9.10_spmd.clone.clone, body=%wide.region_4.9_spmd.clone.clone.sunk | while | flops 552344576 | bytes 37137528 | solution.py:96
  76.7 0.6 dynamic_slice.35
  78.8 8.5 %while.30 = (s32[]{:T(128)}, f32[1,4,512]{2,1,0:T(4,128)S(1)}, f32[1,4,512]{2,1,0:T(4,128)S(1)}, f32[1,4,512,128]{3,2,1,0:T(8,128)S(1)}, s32[]{:T(128)}, /*index...) while((s32[]{:T(128)}, f32[1,4,512]{2,1,0:T(4,128)S(1)}, ...), condition=%wide.region_8.8_spmd, body=%wide.region_5.7_spmd.sunk | while | flops 551819776 | bytes 33433844 | solution.py:91
  78.9 0.3 compare_and_fusion.2
  79.2 2.8 %fusion.29 = (f32[4,512]{1,0:T(4,128)S(1)}, f32[512,512,4]{1,0,2:T(8,128)}) fusion(pred[512,512]{0,1:T(8,128)(4,1)S(1)} %compare_and_fusion.2, bf16[512,1,4,128]{3,0,2,1:T(8,128)(2,1)S(1)} %get-tuple-element.354, bf16[1024,1,256]{2,0,1:T(8,128)(2,1)S(1)} %get-tuple-element.353, s32[]{:T(128)S(6)} %select_n.74), kind=kOutput, calls=%fused_computation.3.clone.1 | convolution fusion | flops 271579136 | bytes 5120004 | tf_op jit(solution)/shard_map/while/body/eval_jaxpr/while/body/qend,ked->enqk/dot_general | solution.py:63
  82.0 4.2 %fusion.32 = f32[1,4,512,128]{3,2,1,0:T(8,128)S(1)} fusion(f32[512,512,4]{1,0,2:T(8,128)} %get-tuple-element.313, f32[4,512]{1,0:T(4,128)S(1)} %bitcast.136, pred[512,512]{0,1:T(8,128)(4,1)S(1)} %compare_and_fusion.2, f32[1,4,512,128]{3,2,1,0:T(8,128)S(1)} %get-tuple-element.333, f32[4,512]{1,0:T(4,128)S(1)} %get-tuple-element.314, ...), kind=kOutput, calls=%fused_computation.10.clone.1 | convolution fusion | flops 274202624 | bytes 6701064 | tf_op jit(solution)/shard_map/while/body/eval_jaxpr/while/body/enqk,ked->enqd/dot_general | solution.py:79
  86.2 1.0 fusion.31
  87.3 1.1 bitcast_dynamic-update-slice_fusion.2
  88.5 0.6 dynamic_slice.35
  90.6 16.9 %while.30 = (s32[]{:T(128)}, f32[1,4,512]{2,1,0:T(4,128)S(1)}, f32[1,4,512]{2,1,0:T(4,128)S(1)}, f32[1,4,512,128]{3,2,1,0:T(8,128)S(1)}, s32[]{:T(128)}, /*index...) while((s32[]{:T(128)}, f32[1,4,512]{2,1,0:T(4,128)S(1)}, ...), condition=%wide.region_8.8_spmd, body=%wide.region_5.7_spmd.sunk | while | flops 551819776 | bytes 33433844 | solution.py:91
  90.7 0.3 compare_and_fusion.2
  90.9 2.8 %fusion.29 = (f32[4,512]{1,0:T(4,128)S(1)}, f32[512,512,4]{1,0,2:T(8,128)}) fusion(pred[512,512]{0,1:T(8,128)(4,1)S(1)} %compare_and_fusion.2, bf16[512,1,4,128]{3,0,2,1:T(8,128)(2,1)S(1)} %get-tuple-element.354, bf16[1024,1,256]{2,0,1:T(8,128)(2,1)S(1)} %get-tuple-element.353, s32[]{:T(128)S(6)} %select_n.74), kind=kOutput, calls=%fused_computation.3.clone.1 | convolution fusion | flops 271579136 | bytes 5120004 | tf_op jit(solution)/shard_map/while/body/eval_jaxpr/while/body/qend,ked->enqk/dot_general | solution.py:63
  93.8 4.2 %fusion.32 = f32[1,4,512,128]{3,2,1,0:T(8,128)S(1)} fusion(f32[512,512,4]{1,0,2:T(8,128)} %get-tuple-element.313, f32[4,512]{1,0:T(4,128)S(1)} %bitcast.136, pred[512,512]{0,1:T(8,128)(4,1)S(1)} %compare_and_fusion.2, f32[1,4,512,128]{3,2,1,0:T(8,128)S(1)} %get-tuple-element.333, f32[4,512]{1,0:T(4,128)S(1)} %get-tuple-element.314, ...), kind=kOutput, calls=%fused_computation.10.clone.1 | convolution fusion | flops 274202624 | bytes 6701064 | tf_op jit(solution)/shard_map/while/body/eval_jaxpr/while/body/enqk,ked->enqd/dot_general | solution.py:79
  98.0 1.0 fusion.31
  99.1 0.3 compare_and_fusion.2
  99.4 2.8 %fusion.29 = (f32[4,512]{1,0:T(4,128)S(1)}, f32[512,512,4]{1,0,2:T(8,128)}) fusion(pred[512,512]{0,1:T(8,128)(4,1)S(1)} %compare_and_fusion.2, bf16[512,1,4,128]{3,0,2,1:T(8,128)(2,1)S(1)} %get-tuple-element.354, bf16[1024,1,256]{2,0,1:T(8,128)(2,1)S(1)} %get-tuple-element.353, s32[]{:T(128)S(6)} %select_n.74), kind=kOutput, calls=%fused_computation.3.clone.1 | convolution fusion | flops 271579136 | bytes 5120004 | tf_op jit(solution)/shard_map/while/body/eval_jaxpr/while/body/qend,ked->enqk/dot_general | solution.py:63
  102.2 4.2 %fusion.32 = f32[1,4,512,128]{3,2,1,0:T(8,128)S(1)} fusion(f32[512,512,4]{1,0,2:T(8,128)} %get-tuple-element.313, f32[4,512]{1,0:T(4,128)S(1)} %bitcast.136, pred[512,512]{0,1:T(8,128)(4,1)S(1)} %compare_and_fusion.2, f32[1,4,512,128]{3,2,1,0:T(8,128)S(1)} %get-tuple-element.333, f32[4,512]{1,0:T(4,128)S(1)} %get-tuple-element.314, ...), kind=kOutput, calls=%fused_computation.10.clone.1 | convolution fusion | flops 274202624 | bytes 6701064 | tf_op jit(solution)/shard_map/while/body/eval_jaxpr/while/body/enqk,ked->enqd/dot_general | solution.py:79
  106.5 1.0 fusion.31
  107.6 1.1 bitcast_dynamic-update-slice_fusion.2
  108.7 3.0 %copy.63 = bf16[1024,1,1,4,128]{4,3,2,1,0:T(4,128)(2,1)} copy(bf16[1024,1,1,4,128]{4,0,3,2,1:T(8,128)(2,1)} %bitcast.147) | data formatting | bytes 2097152 | tf_op jit(solution)/shard_map/reshape;reshape | solution.py:149
  111.7 5.2 %all-to-all-start.2 = ((bf16[1024,1,1,4,128]{4,3,2,1,0:T(4,128)(2,1)}), bf16[1024,1,1,4,128]{4,3,2,1,0:T(4,128)(2,1)S(1)}, u32[]{:S(2)}, u32[]{:S(2)}) async-start(bf16[1024,1,1,4,128]{4,3,2,1,0:T(4,128)(2,1)} %copy.63), calls=%async_computation.2 | async-start | bytes 2097152 | tf_op jit(solution)/shard_map/all_to_all | solution.py:148
  117.0 28.9 %all-to-all-done.2 = bf16[1024,1,1,4,128]{4,3,2,1,0:T(4,128)(2,1)S(1)} async-done(((bf16[1024,1,1,4,128]{4,3,2,1,0:T(4,128)(2,1)}), bf16[1024,1,1,4,128]{4,3,2,1,0:T(4,128)(2,1)S(1)}, u32[]{:S(2)}, u32[]{:S(2)}) %all-to-all-start.2) | async-done | bytes 1048608 | tf_op jit(solution)/shard_map/all_to_all | solution.py:148
  146.1 0.8 copy.65
  146.9 1.6 %reshape.193 = bf16[1,64,8192]{2,1,0:T(8,128)(2,1)} reshape(bf16[64,16,1,1,4,128]{5,4,1,0,3,2:T(4,128)(2,1)S(1)} %copy.65) | data formatting | bytes 2097152 | tf_op jit(solution)/shard_map/reshape | solution.py:156
  148.5 1.7 %copy.95 = bf16[1,1,32,1,16,256]{5,4,3,2,1,0:T(8,128)(2,1)} copy(bf16[1,1,32,1,16,256]{5,4,3,2,1,0:T(8,128)(2,1)} %bitcast.33) | data formatting | bytes 524288
  (50 shorter events, 1.3 us)
Async XLA Ops:
  0.6 15.0 %copy-start.1 = (bf16[1,64,8192]{2,1,0:T(8,128)(2,1)S(1)}, bf16[1,64,8192]{2,1,0:T(8,128)(2,1)}, u32[]{:S(2)}) copy-start(bf16[1,64,8192]{2,1,0:T(8,128)(2,1)} %param.10) | copy-start | bytes 3145732
  6.8 26.0 %all-to-all-start.1 = ((bf16[64,16,1,256]{3,0,2,1:T(8,128)(2,1)}), bf16[64,16,1,256]{3,0,2,1:T(8,128)(2,1)S(1)}, u32[]{:S(2)}, u32[]{:S(2)}) async-start(bf16[64,16,1,256]{3,0,2,1:T(8,128)(2,1)} %bitcast.22), calls=%async_computation.1 | async-start | bytes 1048576 | tf_op jit(solution)/shard_map/all_to_all | solution.py:143
  15.6 1.2 copy-start.2
  32.8 31.8 %all-to-all-start = ((bf16[64,16,1,4,128]{4,0,3,2,1:T(8,128)(2,1)}), bf16[64,16,1,4,128]{4,0,3,2,1:T(8,128)(2,1)S(1)}, u32[]{:S(2)}, u32[]{:S(2)}) async-start(bf16[64,16,1,4,128]{4,0,3,2,1:T(8,128)(2,1)} %maximum_bitcast_fusion), calls=%async_computation | async-start | bytes 2097152 | tf_op jit(solution)/shard_map/all_to_all | solution.py:142
  64.6 47.2 %all-to-all-start.3 = ((bf16[1,1,1,32,16,256]{5,4,2,1,0,3:T(8,128)(2,1)}), bf16[1,1,1,32,16,256]{5,4,2,1,0,3:T(8,128)(2,1)}, u32[]{:S(2)}, u32[]{:S(2)}) async-start(bf16[1,1,1,32,16,256]{5,4,2,1,0,3:T(8,128)(2,1)} %dynamic-slice_bitcast_fusion.4), calls=%async_computation.3 | async-start | bytes 524288 | tf_op jit(solution)/shard_map/all_to_all | solution.py:109
  82.0 4.3 %copy-start = (f32[512,512,4]{1,0,2:T(8,128)S(1)}, f32[512,512,4]{1,0,2:T(8,128)}, u32[]{:S(2)}) copy-start(f32[512,512,4]{1,0,2:T(8,128)} %get-tuple-element.313) | copy-start | bytes 12582916 | tf_op jit(solution)/shard_map/while/body/eval_jaxpr/while
  93.7 4.3 %copy-start = (f32[512,512,4]{1,0,2:T(8,128)S(1)}, f32[512,512,4]{1,0,2:T(8,128)}, u32[]{:S(2)}) copy-start(f32[512,512,4]{1,0,2:T(8,128)} %get-tuple-element.313) | copy-start | bytes 12582916 | tf_op jit(solution)/shard_map/while/body/eval_jaxpr/while
  102.2 4.3 %copy-start = (f32[512,512,4]{1,0,2:T(8,128)S(1)}, f32[512,512,4]{1,0,2:T(8,128)}, u32[]{:S(2)}) copy-start(f32[512,512,4]{1,0,2:T(8,128)} %get-tuple-element.313) | copy-start | bytes 12582916 | tf_op jit(solution)/shard_map/while/body/eval_jaxpr/while
  111.7 34.2 %all-to-all-start.2 = ((bf16[1024,1,1,4,128]{4,3,2,1,0:T(4,128)(2,1)}), bf16[1024,1,1,4,128]{4,3,2,1,0:T(4,128)(2,1)S(1)}, u32[]{:S(2)}, u32[]{:S(2)}) async-start(bf16[1024,1,1,4,128]{4,3,2,1,0:T(4,128)(2,1)} %copy.63), calls=%async_computation.2 | async-start | bytes 2097152 | tf_op jit(solution)/shard_map/all_to_all | solution.py:148
where the time goes:
time: 151 us; the launch traced here: 150 us
  waiting for transfers between devices  66.7 us (44%)
  starting transfers between devices  30.6 us (20%)
  matrix products  21.1 us (14%)
  other arithmetic  14.6 us (10%)
  local copies, waits for them, and re-layouts  13.5 us (9%)
  loops' own time  2.91 us (2%)
    all_to_all x1, waiting for transfers between devices, body(): lax.all_to_all(mixed.reshape(token_count, 1, local_entries, sharing, head...  28.9 us
    all_to_all x1, waiting for transfers between devices, body(): lax.all_to_all(q_split, 'seq', split_axis=1, concat_axis=0, tiled=True)  26.5 us
    dot_general x3, matrix products, key_step(): jnp.einsum('enqk,ked->enqd', weights.astype(jnp.bfloat16), kv_block[...,...  12.7 us
    all_to_all x1, starting transfers between devices, page_cache(): lax.all_to_all(outgoing, 'group', split_axis=3, concat_axis=1, tiled=True)  12 us
    all_to_all x1, waiting for transfers between devices, body(): lax.all_to_all(spread, 'seq', split_axis=1, concat_axis=0, tiled=True)  11.3 us
    all_to_all x1, starting transfers between devices, body(): lax.all_to_all(spread, 'seq', split_axis=1, concat_axis=0, tiled=True)  8.77 us
    dot_general x3, matrix products, key_step(): jnp.einsum('qend,ked->enqk', q_block, kv_block[..., :head_width], preferr...  8.42 us
    all_to_all x1, starting transfers between devices, body(): lax.all_to_all(mixed.reshape(token_count, 1, local_entries, sharing, head...  5.24 us
  transfers between devices with their start and end apart: 4, of which 3 were waited for; matrix products, arithmetic and copies ran while one was open for 26% of the time, Pallas kernels for 0%

commit v1 on v0

--- a/solution.py
+++ b/solution.py
@@ -8,6 +8,12 @@
 NORM_EPS = 1e-06
 ROPE_BASE = 1000000.0
 MASKED = -1e30
+
+
+def exchange_blocks(x, name, split, join):
+    pieces = jnp.split(x, lax.axis_size(name), axis=split)
+    incoming = lax.all_to_all(jnp.stack(pieces), name, 0, 0)
+    return jnp.concatenate(incoming, axis=join)
 
 
 def token_starts(lengths, count):
@@ -145,12 +151,8 @@
     q_all = q_got.reshape(token_count, local_entries, sharing, head_width)
     kv_all = kv_got.reshape(token_count, local_entries, 2 * head_width)
     mixed = attend(q_all, kv_all, starts, head_width)
-    back = lax.all_to_all(
-        mixed.reshape(token_count, 1, local_entries, sharing, head_width),
-        "seq",
-        split_axis=0,
-        concat_axis=1,
-        tiled=True,
+    back = exchange_blocks(
+        mixed.reshape(token_count, 1, local_entries, sharing, head_width), "seq", 0, 1
     )
     cache = page_cache(kv_all, entry_first, repeat)
     attended = back.reshape(1, row_count, q_heads * head_width)

time: 151 us -> 172 us (1.14)
  local copies, waits for them, and re-layouts: 13.5 us -> 33.9 us
    unnamed x8 -> x23, local copies, waits for them, and re-layouts: 3.04 us -> 25.1 us
    another operation x9 -> x10, local copies, waits for them, and re-layouts: 4.53 us -> 4.6 us  [the longest x1 1.61 us: body(): attended = back.reshape(1, row_count, q_heads * head_width)]
  transfers between devices with their start and end apart: 4 -> 4, of which waited for: 3 -> 3; matrix products, arithmetic and copies ran while one was open for 26% -> 35% of each run, Pallas kernels for 0% -> 0%
where the time goes in v1:
time: 172 us; the launch traced here: 171 us
  waiting for transfers between devices  66.7 us (39%)
  local copies, waits for them, and re-layouts  33.9 us (20%)
  starting transfers between devices  30.5 us (18%)
  matrix products  21.1 us (12%)
  other arithmetic  14.6 us (8%)
  loops' own time  2.91 us (2%)
    all_to_all x1, waiting for transfers between devices, exchange_blocks(): incoming = lax.all_to_all(jnp.stack(pieces), name, 0, 0)  28.9 us
    all_to_all x1, waiting for transfers between devices, body(): lax.all_to_all(q_split, 'seq', split_axis=1, concat_axis=0, tiled=True)  26.5 us
    unnamed x23, local copies, waits for them, and re-layouts  25.1 us
    dot_general x3, matrix products, key_step(): jnp.einsum('enqk,ked->enqd', weights.astype(jnp.bfloat16), kv_block[...,...  12.7 us
    all_to_all x1, starting transfers between devices, page_cache(): lax.all_to_all(outgoing, 'group', split_axis=3, concat_axis=1, tiled=True)  12 us
    all_to_all x1, waiting for transfers between devices, body(): lax.all_to_all(spread, 'seq', split_axis=1, concat_axis=0, tiled=True)  11.3 us
    all_to_all x1, starting transfers between devices, body(): lax.all_to_all(spread, 'seq', split_axis=1, concat_axis=0, tiled=True)  8.77 us
    dot_general x3, matrix products, key_step(): jnp.einsum('qend,ked->enqk', q_block, kv_block[..., :head_width], preferr...  8.43 us
  transfers between devices with their start and end apart: 4, of which 3 were waited for; matrix products, arithmetic and copies ran while one was open for 35% of the time, Pallas kernels for 0%

profile of v1, /device:TPU:2, one launch (start us, length us, event | category | flops | bytes accessed | tf_op | source)
XLA Modules:
  0.0 170.5 jit_solution(2355273898970478362)
XLA Ops:
  0.7 0.9 reduce-window.8
  1.6 0.9 convert_bitcast_fusion.1
  2.9 0.9 copy.79
  4.8 0.8 multiply_multiply_fusion.1
  6.0 0.9 broadcast_in_dim.18
  6.8 8.8 %all-to-all-start.1 = ((bf16[64,16,1,256]{3,0,2,1:T(8,128)(2,1)}), bf16[64,16,1,256]{3,0,2,1:T(8,128)(2,1)S(1)}, u32[]{:S(2)}, u32[]{:S(2)}) async-start(bf16[64,16,1,256]{3,0,2,1:T(8,128)(2,1)} %bitcast.22), calls=%async_computation.1 | async-start | bytes 1048576 | tf_op jit(solution)/shard_map/all_to_all | solution.py:149
  16.8 0.9 multiply_multiply_fusion
  17.7 0.9 subtract_convert_fusion
  20.0 1.6 maximum_bitcast_fusion
  21.6 11.3 %all-to-all-done.1 = bf16[64,16,1,256]{3,0,2,1:T(8,128)(2,1)S(1)} async-done(((bf16[64,16,1,256]{3,0,2,1:T(8,128)(2,1)}), bf16[64,16,1,256]{3,0,2,1:T(8,128)(2,1)S(1)}, u32[]{:S(2)}, u32[]{:S(2)}) %all-to-all-start.1) | async-done | bytes 524320 | tf_op jit(solution)/shard_map/all_to_all | solution.py:149
  32.8 4.5 %all-to-all-start = ((bf16[64,16,1,4,128]{4,0,3,2,1:T(8,128)(2,1)}), bf16[64,16,1,4,128]{4,0,3,2,1:T(8,128)(2,1)S(1)}, u32[]{:S(2)}, u32[]{:S(2)}) async-start(bf16[64,16,1,4,128]{4,0,3,2,1:T(8,128)(2,1)} %maximum_bitcast_fusion), calls=%async_computation | async-start | bytes 2097152 | tf_op jit(solution)/shard_map/all_to_all | solution.py:148
  38.1 26.5 %all-to-all-done = bf16[64,16,1,4,128]{4,0,3,2,1:T(8,128)(2,1)S(1)} async-done(((bf16[64,16,1,4,128]{4,0,3,2,1:T(8,128)(2,1)}), bf16[64,16,1,4,128]{4,0,3,2,1:T(8,128)(2,1)S(1)}, u32[]{:S(2)}, u32[]{:S(2)}) %all-to-all-start) | async-done | bytes 1048608 | tf_op jit(solution)/shard_map/all_to_all | solution.py:148
  64.6 12.0 %all-to-all-start.3 = ((bf16[1,1,1,32,16,256]{5,4,2,1,0,3:T(8,128)(2,1)}), bf16[1,1,1,32,16,256]{5,4,2,1,0,3:T(8,128)(2,1)}, u32[]{:S(2)}, u32[]{:S(2)}) async-start(bf16[1,1,1,32,16,256]{5,4,2,1,0,3:T(8,128)(2,1)} %dynamic-slice_bitcast_fusion.4), calls=%async_computation.3 | async-start | bytes 524288 | tf_op jit(solution)/shard_map/all_to_all | solution.py:115
  76.7 32.0 %while.29 = (s32[]{:T(128)}, bf16[2,512,1,4,128]{4,1,0,3,2:T(8,128)(2,1)}, s32[2]{0:T(128)S(1)}, bf16[1024,1,4,128]{3,0,2,1:T(8,128)(2,1)S(1)}, s32[1024]{0:T(10...) while((s32[]{:T(128)}, ...), condition=%wide.region_9.10_spmd.clone.clone, body=%wide.region_4.9_spmd.clone.clone.sunk | while | flops 552344576 | bytes 37137528 | solution.py:102
  78.8 8.5 %while.30 = (s32[]{:T(128)}, f32[1,4,512]{2,1,0:T(4,128)S(1)}, f32[1,4,512]{2,1,0:T(4,128)S(1)}, f32[1,4,512,128]{3,2,1,0:T(8,128)S(1)}, s32[]{:T(128)}, /*index...) while((s32[]{:T(128)}, f32[1,4,512]{2,1,0:T(4,128)S(1)}, ...), condition=%wide.region_8.8_spmd, body=%wide.region_5.7_spmd.sunk | while | flops 551819776 | bytes 33433844 | solution.py:97
  79.2 2.8 %fusion.45 = (f32[4,512]{1,0:T(4,128)S(1)}, f32[512,512,4]{1,0,2:T(8,128)}) fusion(pred[512,512]{0,1:T(8,128)(4,1)S(1)} %compare_and_fusion.2, bf16[512,1,4,128]{3,0,2,1:T(8,128)(2,1)S(1)} %get-tuple-element.354, bf16[1024,1,256]{2,0,1:T(8,128)(2,1)S(1)} %get-tuple-element.353, s32[]{:T(128)S(6)} %select_n.74), kind=kOutput, calls=%fused_computation.3.clone.1 | convolution fusion | flops 271579136 | bytes 5120004 | tf_op jit(solution)/shard_map/while/body/eval_jaxpr/while/body/qend,ked->enqk/dot_general | solution.py:69
  82.0 4.2 %fusion.48 = f32[1,4,512,128]{3,2,1,0:T(8,128)S(1)} fusion(f32[512,512,4]{1,0,2:T(8,128)} %get-tuple-element.313, f32[4,512]{1,0:T(4,128)S(1)} %bitcast.198, pred[512,512]{0,1:T(8,128)(4,1)S(1)} %compare_and_fusion.2, f32[1,4,512,128]{3,2,1,0:T(8,128)S(1)} %get-tuple-element.333, f32[4,512]{1,0:T(4,128)S(1)} %get-tuple-element.314, ...), kind=kOutput, calls=%fused_computation.10.clone.1 | convolution fusion | flops 274202624 | bytes 6701064 | tf_op jit(solution)/shard_map/while/body/eval_jaxpr/while/body/enqk,ked->enqd/dot_general | solution.py:85
  86.2 1.0 fusion.47
  87.3 1.1 bitcast_dynamic-update-slice_fusion.2
  90.6 17.0 %while.30 = (s32[]{:T(128)}, f32[1,4,512]{2,1,0:T(4,128)S(1)}, f32[1,4,512]{2,1,0:T(4,128)S(1)}, f32[1,4,512,128]{3,2,1,0:T(8,128)S(1)}, s32[]{:T(128)}, /*index...) while((s32[]{:T(128)}, f32[1,4,512]{2,1,0:T(4,128)S(1)}, ...), condition=%wide.region_8.8_spmd, body=%wide.region_5.7_spmd.sunk | while | flops 551819776 | bytes 33433844 | solution.py:97
  90.9 2.8 %fusion.45 = (f32[4,512]{1,0:T(4,128)S(1)}, f32[512,512,4]{1,0,2:T(8,128)}) fusion(pred[512,512]{0,1:T(8,128)(4,1)S(1)} %compare_and_fusion.2, bf16[512,1,4,128]{3,0,2,1:T(8,128)(2,1)S(1)} %get-tuple-element.354, bf16[1024,1,256]{2,0,1:T(8,128)(2,1)S(1)} %get-tuple-element.353, s32[]{:T(128)S(6)} %select_n.74), kind=kOutput, calls=%fused_computation.3.clone.1 | convolution fusion | flops 271579136 | bytes 5120004 | tf_op jit(solution)/shard_map/while/body/eval_jaxpr/while/body/qend,ked->enqk/dot_general | solution.py:69
  93.8 4.2 %fusion.48 = f32[1,4,512,128]{3,2,1,0:T(8,128)S(1)} fusion(f32[512,512,4]{1,0,2:T(8,128)} %get-tuple-element.313, f32[4,512]{1,0:T(4,128)S(1)} %bitcast.198, pred[512,512]{0,1:T(8,128)(4,1)S(1)} %compare_and_fusion.2, f32[1,4,512,128]{3,2,1,0:T(8,128)S(1)} %get-tuple-element.333, f32[4,512]{1,0:T(4,128)S(1)} %get-tuple-element.314, ...), kind=kOutput, calls=%fused_computation.10.clone.1 | convolution fusion | flops 274202624 | bytes 6701064 | tf_op jit(solution)/shard_map/while/body/eval_jaxpr/while/body/enqk,ked->enqd/dot_general | solution.py:85
  98.0 1.0 fusion.47
  99.4 2.8 %fusion.45 = (f32[4,512]{1,0:T(4,128)S(1)}, f32[512,512,4]{1,0,2:T(8,128)}) fusion(pred[512,512]{0,1:T(8,128)(4,1)S(1)} %compare_and_fusion.2, bf16[512,1,4,128]{3,0,2,1:T(8,128)(2,1)S(1)} %get-tuple-element.354, bf16[1024,1,256]{2,0,1:T(8,128)(2,1)S(1)} %get-tuple-element.353, s32[]{:T(128)S(6)} %select_n.74), kind=kOutput, calls=%fused_computation.3.clone.1 | convolution fusion | flops 271579136 | bytes 5120004 | tf_op jit(solution)/shard_map/while/body/eval_jaxpr/while/body/qend,ked->enqk/dot_general | solution.py:69
  102.2 4.2 %fusion.48 = f32[1,4,512,128]{3,2,1,0:T(8,128)S(1)} fusion(f32[512,512,4]{1,0,2:T(8,128)} %get-tuple-element.313, f32[4,512]{1,0:T(4,128)S(1)} %bitcast.198, pred[512,512]{0,1:T(8,128)(4,1)S(1)} %compare_and_fusion.2, f32[1,4,512,128]{3,2,1,0:T(8,128)S(1)} %get-tuple-element.333, f32[4,512]{1,0:T(4,128)S(1)} %get-tuple-element.314, ...), kind=kOutput, calls=%fused_computation.10.clone.1 | convolution fusion | flops 274202624 | bytes 6701064 | tf_op jit(solution)/shard_map/while/body/eval_jaxpr/while/body/enqk,ked->enqd/dot_general | solution.py:85
  106.5 1.0 fusion.47
  107.6 1.1 bitcast_dynamic-update-slice_fusion.2
  108.7 1.5 fusion.38
  110.2 1.5 fusion.37
  111.6 1.5 fusion.36
  113.1 1.5 fusion.35
  114.6 1.5 fusion.34
  116.1 1.5 fusion.33
  117.5 1.5 fusion.32
  119.0 1.5 fusion.31
  120.4 1.5 fusion.30
  121.9 1.5 fusion.29
  123.4 1.5 fusion.28
  124.9 1.5 fusion.27
  126.3 1.5 fusion.26
  127.8 1.5 fusion.25
  129.3 1.5 fusion.24
  130.8 1.5 fusion.23
  132.2 5.2 %all-to-all-start.2 = ((bf16[16,64,1,1,4,128]{5,1,4,3,2,0:T(8,128)(2,1)}), bf16[16,64,1,1,4,128]{5,1,4,3,2,0:T(8,128)(2,1)S(1)}, u32[]{:S(2)}, u32[]{:S(2)}) async-start(bf16[16,64,1,1,4,128]{5,1,4,3,2,0:T(8,128)(2,1)} %fusion.23), calls=%async_computation.2 | async-start | bytes 2097152 | tf_op jit(solution)/shard_map/all_to_all | solution.py:15
  137.5 28.9 %all-to-all-done.2 = bf16[16,64,1,1,4,128]{5,1,4,3,2,0:T(8,128)(2,1)S(1)} async-done(((bf16[16,64,1,1,4,128]{5,1,4,3,2,0:T(8,128)(2,1)}), bf16[16,64,1,1,4,128]{5,1,4,3,2,0:T(8,128)(2,1)S(1)}, u32[]{:S(2)}, u32[]{:S(2)}) %all-to-all-start.2) | async-done | bytes 1048608 | tf_op jit(solution)/shard_map/all_to_all | solution.py:15
  166.4 0.8 copy.72
  167.2 1.6 reshape_reshape.14
  168.8 1.7 copy.117
  (64 shorter events, 7.6 us)
Async XLA Ops:
  0.6 15.0 %copy-start.1 = (bf16[1,64,8192]{2,1,0:T(8,128)(2,1)S(1)}, bf16[1,64,8192]{2,1,0:T(8,128)(2,1)}, u32[]{:S(2)}) copy-start(bf16[1,64,8192]{2,1,0:T(8,128)(2,1)} %param.10) | copy-start | bytes 3145732
  6.8 26.0 %all-to-all-start.1 = ((bf16[64,16,1,256]{3,0,2,1:T(8,128)(2,1)}), bf16[64,16,1,256]{3,0,2,1:T(8,128)(2,1)S(1)}, u32[]{:S(2)}, u32[]{:S(2)}) async-start(bf16[64,16,1,256]{3,0,2,1:T(8,128)(2,1)} %bitcast.22), calls=%async_computation.1 | async-start | bytes 1048576 | tf_op jit(solution)/shard_map/all_to_all | solution.py:149
  15.6 1.2 copy-start.2
  32.8 31.8 %all-to-all-start = ((bf16[64,16,1,4,128]{4,0,3,2,1:T(8,128)(2,1)}), bf16[64,16,1,4,128]{4,0,3,2,1:T(8,128)(2,1)S(1)}, u32[]{:S(2)}, u32[]{:S(2)}) async-start(bf16[64,16,1,4,128]{4,0,3,2,1:T(8,128)(2,1)} %maximum_bitcast_fusion), calls=%async_computation | async-start | bytes 2097152 | tf_op jit(solution)/shard_map/all_to_all | solution.py:148
  64.6 67.6 %all-to-all-start.3 = ((bf16[1,1,1,32,16,256]{5,4,2,1,0,3:T(8,128)(2,1)}), bf16[1,1,1,32,16,256]{5,4,2,1,0,3:T(8,128)(2,1)}, u32[]{:S(2)}, u32[]{:S(2)}) async-start(bf16[1,1,1,32,16,256]{5,4,2,1,0,3:T(8,128)(2,1)} %dynamic-slice_bitcast_fusion.4), calls=%async_computation.3 | async-start | bytes 524288 | tf_op jit(solution)/shard_map/all_to_all | solution.py:115
  82.0 4.3 %copy-start = (f32[512,512,4]{1,0,2:T(8,128)S(1)}, f32[512,512,4]{1,0,2:T(8,128)}, u32[]{:S(2)}) copy-start(f32[512,512,4]{1,0,2:T(8,128)} %get-tuple-element.313) | copy-start | bytes 12582916 | tf_op jit(solution)/shard_map/while/body/eval_jaxpr/while
  93.7 4.3 %copy-start = (f32[512,512,4]{1,0,2:T(8,128)S(1)}, f32[512,512,4]{1,0,2:T(8,128)}, u32[]{:S(2)}) copy-start(f32[512,512,4]{1,0,2:T(8,128)} %get-tuple-element.313) | copy-start | bytes 12582916 | tf_op jit(solution)/shard_map/while/body/eval_jaxpr/while
  102.2 4.3 %copy-start = (f32[512,512,4]{1,0,2:T(8,128)S(1)}, f32[512,512,4]{1,0,2:T(8,128)}, u32[]{:S(2)}) copy-start(f32[512,512,4]{1,0,2:T(8,128)} %get-tuple-element.313) | copy-start | bytes 12582916 | tf_op jit(solution)/shard_map/while/body/eval_jaxpr/while
  132.2 34.2 %all-to-all-start.2 = ((bf16[16,64,1,1,4,128]{5,1,4,3,2,0:T(8,128)(2,1)}), bf16[16,64,1,1,4,128]{5,1,4,3,2,0:T(8,128)(2,1)S(1)}, u32[]{:S(2)}, u32[]{:S(2)}) async-start(bf16[16,64,1,1,4,128]{5,1,4,3,2,0:T(8,128)(2,1)} %fusion.23), calls=%async_computation.2 | async-start | bytes 2097152 | tf_op jit(solution)/shard_map/all_to_all | solution.py:15
